TPU v7x, 32 devices: a whole 2x2x4 slice. The times are simulated.
32 devices in a mesh: groups: 2 (over y), seg: 16 (over z, x, core).
Axes of the slice: x: 2, y: 2, z: 4, core: 2. Of those that a mesh axis runs over, the one named last changes fastest.
Arguments:
- queries: bfloat16 [16384, 4096], P(('groups', 'seg')), parts along dimension 0, may hold values from -320 to 320
- keys: bfloat16 [16384, 1024], P(('groups', 'seg')), parts along dimension 0, may hold values from -60 to 60
- values: bfloat16 [16384, 1024], P(('groups', 'seg')), parts along dimension 0, may hold values from -14 to 14
Outputs:
- attended: bfloat16 [16384, 4096], P(('groups', 'seg')), parts along dimension 0
There are 2 independent parts, one for each index of `groups`. A program takes and returns all parts, laid end to end along the dimension named above; each array names one. Nothing has to cross between parts.
All inputs are finite; a program needn't handle non-finite values.
Results may differ from a plain program's by a relative error of at most 0.0036.
Values may be sent and summed in bfloat16 or wider, within the bound.
A program may use at most 128 MiB of HBM per device.

v0:
```python
import math

import jax
import jax.numpy as jnp
from jax import lax
from jax.sharding import PartitionSpec as P

QH = 32
KVH = 8
DH = 128


def partner(array, axis, distance):
    return lax.ppermute(array, axis, [(i, i ^ 1 << distance) for i in range(lax.axis_size(axis))])


def entering(array, axis, combine, identity):
    count, mine = (lax.axis_size(axis), lax.axis_index(axis))
    everything = jax.tree.map(
        lambda part, kind: lax.all_gather(part.astype(kind), axis),
        array,
        (jnp.bfloat16, jnp.bfloat16),
    )
    start = jax.tree.map(
        lambda part, zero: jnp.broadcast_to(jnp.asarray(zero, part.dtype), part.shape),
        array,
        identity,
    )

    def step(k, before):
        reached = k < mine
        new = combine(
            before, jax.tree.map(lambda part, own: part[k].astype(own.dtype), everything, array)
        )
        return jax.tree.map(lambda a, b: jnp.where(reached, a, b), new, before)

    return lax.fori_loop(0, count, step, start)


def features(block):
    return (jax.nn.elu(block.astype(jnp.float32)) + 1.0).astype(jnp.bfloat16)


def memory_terms(key_rows, value_rows):
    tok_rows = key_rows.shape[0]
    head_count = key_rows.shape[1] // DH
    key_feat = features(key_rows).reshape(tok_rows, head_count, DH)
    value_heads = value_rows.reshape(tok_rows, head_count, DH)
    memory_delta = jnp.einsum(
        "thd,the->hde", key_feat, value_heads, preferred_element_type=jnp.float32
    )
    norm_delta = jnp.sum(key_feat.astype(jnp.float32), axis=0)
    return (memory_delta, norm_delta)


def combine(earlier, later):
    return (earlier[0] + later[0], earlier[1] + later[1])


def on_device(queries, keys, values):
    tok_rows = queries.shape[0]
    seg_rows = 2 * tok_rows
    group_size = QH // KVH
    col_width = group_size * DH
    half_heads = KVH // 2
    query_half = half_heads * col_width
    key_half = half_heads * DH
    parity_odd = lax.axis_index("seg") % 2
    is_odd = parity_odd == 1
    query_mine = lax.dynamic_slice_in_dim(queries, parity_odd * query_half, query_half, 1)
    query_send = lax.dynamic_slice_in_dim(queries, (1 - parity_odd) * query_half, query_half, 1)
    key_mine = lax.dynamic_slice_in_dim(keys, parity_odd * key_half, key_half, 1)
    key_send = lax.dynamic_slice_in_dim(keys, (1 - parity_odd) * key_half, key_half, 1)
    value_mine = lax.dynamic_slice_in_dim(values, parity_odd * key_half, key_half, 1)
    value_send = lax.dynamic_slice_in_dim(values, (1 - parity_odd) * key_half, key_half, 1)
    query_got, key_got, value_got = partner((query_send, key_send, value_send), "seg", 0)
    query_full = jnp.concatenate(
        [jnp.where(is_odd, query_got, query_mine), jnp.where(is_odd, query_mine, query_got)], 0
    )
    key_full = jnp.concatenate(
        [jnp.where(is_odd, key_got, key_mine), jnp.where(is_odd, key_mine, key_got)], 0
    )
    value_full = jnp.concatenate(
        [jnp.where(is_odd, value_got, value_mine), jnp.where(is_odd, value_mine, value_got)], 0
    )
    seg_delta, seg_norm = memory_terms(key_full, value_full)
    padded_delta = lax.dynamic_update_slice_in_dim(
        jnp.zeros((KVH, DH, DH), jnp.float32), seg_delta, parity_odd * half_heads, 0
    )
    padded_norm = lax.dynamic_update_slice_in_dim(
        jnp.zeros((KVH, DH), jnp.float32), seg_norm, parity_odd * half_heads, 0
    )
    before_mem, before_norm = entering(
        (padded_delta, padded_norm),
        "seg",
        combine,
        (jnp.zeros_like(padded_delta), jnp.zeros_like(padded_norm)),
    )
    memory = lax.dynamic_slice_in_dim(before_mem, parity_odd * half_heads, half_heads, 0)
    norm_sum = lax.dynamic_slice_in_dim(before_norm, parity_odd * half_heads, half_heads, 0)
    positions = jnp.arange(seg_rows)
    allowed = positions[None, :] <= positions[:, None]

    def head_group(head_index, output):
        query_block = lax.dynamic_slice_in_dim(
            query_full, head_index * col_width, col_width, 1
        ).reshape(seg_rows, group_size, DH)
        key_block = lax.dynamic_slice_in_dim(key_full, head_index * DH, DH, 1)
        value_block = lax.dynamic_slice_in_dim(value_full, head_index * DH, DH, 1)
        scores = jnp.einsum(
            "tjd,ud->jtu", query_block, key_block, preferred_element_type=jnp.float32
        ) / math.sqrt(DH)
        scores = jnp.where(allowed[None], scores, -1e30)
        row_max = jnp.max(scores, axis=-1, keepdims=True)
        weights_raw = jnp.exp(scores - row_max)
        row_total = jnp.sum(weights_raw, axis=-1, keepdims=True)
        weights = (weights_raw / row_total).astype(jnp.bfloat16)
        local_out = jnp.einsum(
            "jtu,ud->tjd", weights, value_block, preferred_element_type=jnp.float32
        )
        query_feat = features(query_block).astype(jnp.float32)
        mem_head = memory[head_index]
        norm_head = norm_sum[head_index]
        numerator = jnp.einsum("tjd,de->tje", query_feat, mem_head, precision=lax.Precision.HIGHEST)
        denominator = jnp.einsum(
            "tjd,d->tj", query_feat, norm_head, precision=lax.Precision.HIGHEST
        )
        mem_read = numerator / jnp.maximum(denominator, 1.0)[..., None]
        out_block = (0.5 * (local_out + mem_read)).astype(jnp.bfloat16).reshape(seg_rows, col_width)
        return lax.dynamic_update_slice_in_dim(output, out_block, head_index * col_width, 1)

    joined = lax.fori_loop(
        0, half_heads, head_group, jnp.zeros((seg_rows, query_half), jnp.bfloat16)
    )
    first_rows = joined[:tok_rows]
    second_rows = joined[tok_rows:]
    keep_rows = jnp.where(is_odd, second_rows, first_rows)
    send_rows = jnp.where(is_odd, first_rows, second_rows)
    got_rows = partner(send_rows, "seg", 0)
    left_cols = jnp.where(is_odd, got_rows, keep_rows)
    right_cols = jnp.where(is_odd, keep_rows, got_rows)
    return jnp.concatenate([left_cols, right_cols], 1)


def solution(mesh):
    return jax.shard_map(
        on_device,
        mesh=mesh,
        in_specs=(
            P(("groups", "seg"), None),
            P(("groups", "seg"), None),
            P(("groups", "seg"), None),
        ),
        out_specs=P(("groups", "seg"), None),
        check_vma=False,
    )
```

profile of v0, /device:TPU:0, one launch (start us, length us, event | category | flops | bytes accessed | tf_op | source)
XLA Modules:
  0.0 208.7 jit_solution(18167903505648442048)
XLA Ops:
  6.5 1.7 constant_dynamic-slice_fusion.6
  14.5 3.2 %constant_dynamic-slice_fusion.4 = bf16[512,2048]{1,0:T(8,128)(2,1)} fusion(bf16[512,4096]{1,0:T(8,128)(2,1)} %param.7, s32[]{:T(128)S(6)} %select_n.190), kind=kLoop, calls=%fused_computation.68 | loop fusion | bytes 4194308 | tf_op jit(solution)/shard_map/dynamic_slice | solution.py:71
  19.0 23.1 %all-gather.1 = bf16[128,128]{1,0:T(8,128)(2,1)S(1)} all-gather(bf16[8,128]{1,0:T(8,128)(2,1)S(1)} %constant_dynamic-update-slice_fusion.1), channel_id=3, replica_groups=mesh['groups'=2,'seg'=16] {'seg'}, dimensions={0}, use_global_device_ids=true | all-gather | bytes 34816 | tf_op jit(solution)/shard_map/all_gather | solution.py:20
  42.3 4.1 %broadcast_select_fusion.5 = (bf16[512,2048]{1,0:T(8,128)(2,1)S(1)}, bf16[512,2048]{1,0:T(8,128)(2,1)S(1)}) fusion(bf16[512,2048]{1,0:T(8,128)(2,1)} %collective-permute-done.2, pred[]{:T(512)S(6)} %eq.5, bf16[512,4096]{1,0:T(8,128)(2,1)} %param.7, s32[]{:T(128)S(6)} %select_n.191), kind=kLoop, calls=%fused_computation.57 | loop fusion | flops 2097152 | bytes 8388613 | tf_op jit(solution)/shard_map/jit(_where)/select_n | solution.py:78
  46.4 2.5 %pad_maximum_fusion = bf16[1024,2048]{1,0:T(8,128)(2,1)} fusion(bf16[512,2048]{1,0:T(8,128)(2,1)S(1)} %get-tuple-element.346, bf16[512,2048]{1,0:T(8,128)(2,1)S(1)} %get-tuple-element.345), kind=kLoop, calls=%fused_computation.46 | loop fusion | flops 8388608 | bytes 8388608 | tf_op jit(solution)/shard_map/concatenate | solution.py:77
  48.9 18.9 %all-gather.4.cloned.1.call-done = bf16[128,128,128]{2,1,0:T(8,128)(2,1)} async-done(((bf16[8,128,128]{2,1,0:T(8,128)(2,1)}), bf16[128,128,128]{2,1,0:T(8,128)(2,1)}) %all-gather.4.cloned.1.call-update) | async-done | bytes 4194320 | tf_op jit(solution)/shard_map/all_gather | solution.py:20
  67.9 20.4 %while.31 = (s32[]{:T(128)}, f32[8,128,128]{2,1,0:T(8,128)S(1)}, f32[8,128]{1,0:T(8,128)S(1)}, s32[]{:T(128)}, bf16[16,8,128,128]{3,2,1,0:T(8,128)(2,1)}, /*inde...) while((s32[]{:T(128)}, f32[8,128,128]{2,1,0:T(8,128)S(1)}, f32[8,128]{1,0:T(8,128)S(1)}, ...), condition=%wide.region_2.3_spmd.clone, body=%wide.region_1.2_spmd.clone.sunk | while | flops 528388 | bytes 1321075 | solution.py:37
  69.1 1.2 add_select_fusion.4
  70.4 1.2 add_select_fusion.4
  71.7 1.2 add_select_fusion.4
  73.0 1.2 add_select_fusion.4
  88.3 2.5 %broadcast_in_dim.47.clone = bf16[1024,2048]{1,0:T(8,128)(2,1)} broadcast(bf16[]{:T(256)} %constant.138.clone.1), dimensions={} | broadcast | bytes 4194306 | tf_op jit(solution)/shard_map/broadcast_in_dim | solution.py:133
  90.9 101.3 %while.30 = (s32[]{:T(128)}, bf16[1024,2048]{1,0:T(8,128)(2,1)}, bf16[1024,512]{0,1:T(8,128)(2,1)}, bf16[1024,512]{0,1:T(8,128)(2,1)S(1)}, bf16[1024,2048]{1,0:T...) while((s32[]{:T(128)}, bf16[1024,2048]{1,0:T(8,128)(2,1)}, ...), condition=%wide.region_6.7_spmd.clone, body=%wide.region_3.6_spmd.clone.sunk | while | flops 2990543872 | bytes 63636256 | solution.py:132
  90.9 1.7 constant_dynamic-slice_fusion.10
  93.4 9.7 %fusion.77 = (f32[4,1024]{1,0:T(4,128)S(1)}, f32[4,1024,1024]{1,2,0:T(8,128)}) fusion(pred[1024,1024]{0,1:T(8,128)(4,1)S(1)} %iota_compare_fusion.2, bf16[1024,4,128]{0,2,1:T(8,128)(2,1)S(1)} %bitcast.97, bf16[1024,512]{0,1:T(8,128)(2,1)S(1)} %get-tuple-element.492, s32[]{:T(128)S(6)} %select_n.299), kind=kOutput, calls=%fused_computation.73.clone.1 | convolution fusion | flops 1090520064 | bytes 19152900 | tf_op jit(solution)/shard_map/while/body/eval_jaxpr/sub | solution.py:115
  105.9 1.3 fusion.76
  107.2 7.4 %fusion.79 = bf16[1024,4,128]{0,2,1:T(8,128)(2,1)S(1)} fusion(f32[1024,4,128]{0,2,1:T(8,128)S(1)} %fusion.76, f32[4,1024,1024]{1,2,0:T(8,128)} %get-tuple-element.433, f32[4,1024]{1,0:T(4,128)S(1)} %get-tuple-element.434, f32[1024,4]{0,1:T(4,128)S(1)} %bitcast_maximum_fusion.2, bf16[1024,512]{0,1:T(8,128)(2,1)} %get-tuple-element.491, s32[]{:T(128)S(6)} %select_n.299), kind=kOutput, calls=%fused_computation.18.clone.1 | convolution fusion | flops 1084227584 | bytes 20217860 | tf_op jit(solution)/shard_map/while/body/eval_jaxpr/jtu,ud->tjd/dot_general | solution.py:118
  116.2 1.7 constant_dynamic-slice_fusion.10
  118.8 9.7 %fusion.77 = (f32[4,1024]{1,0:T(4,128)S(1)}, f32[4,1024,1024]{1,2,0:T(8,128)}) fusion(pred[1024,1024]{0,1:T(8,128)(4,1)S(1)} %iota_compare_fusion.2, bf16[1024,4,128]{0,2,1:T(8,128)(2,1)S(1)} %bitcast.97, bf16[1024,512]{0,1:T(8,128)(2,1)S(1)} %get-tuple-element.492, s32[]{:T(128)S(6)} %select_n.299), kind=kOutput, calls=%fused_computation.73.clone.1 | convolution fusion | flops 1090520064 | bytes 19152900 | tf_op jit(solution)/shard_map/while/body/eval_jaxpr/sub | solution.py:115
  131.2 1.3 fusion.76
  132.5 7.4 %fusion.79 = bf16[1024,4,128]{0,2,1:T(8,128)(2,1)S(1)} fusion(f32[1024,4,128]{0,2,1:T(8,128)S(1)} %fusion.76, f32[4,1024,1024]{1,2,0:T(8,128)} %get-tuple-element.433, f32[4,1024]{1,0:T(4,128)S(1)} %get-tuple-element.434, f32[1024,4]{0,1:T(4,128)S(1)} %bitcast_maximum_fusion.2, bf16[1024,512]{0,1:T(8,128)(2,1)} %get-tuple-element.491, s32[]{:T(128)S(6)} %select_n.299), kind=kOutput, calls=%fused_computation.18.clone.1 | convolution fusion | flops 1084227584 | bytes 20217860 | tf_op jit(solution)/shard_map/while/body/eval_jaxpr/jtu,ud->tjd/dot_general | solution.py:118
  141.5 1.7 constant_dynamic-slice_fusion.10
  144.1 9.7 %fusion.77 = (f32[4,1024]{1,0:T(4,128)S(1)}, f32[4,1024,1024]{1,2,0:T(8,128)}) fusion(pred[1024,1024]{0,1:T(8,128)(4,1)S(1)} %iota_compare_fusion.2, bf16[1024,4,128]{0,2,1:T(8,128)(2,1)S(1)} %bitcast.97, bf16[1024,512]{0,1:T(8,128)(2,1)S(1)} %get-tuple-element.492, s32[]{:T(128)S(6)} %select_n.299), kind=kOutput, calls=%fused_computation.73.clone.1 | convolution fusion | flops 1090520064 | bytes 19152900 | tf_op jit(solution)/shard_map/while/body/eval_jaxpr/sub | solution.py:115
  156.6 1.3 fusion.76
  157.8 7.4 %fusion.79 = bf16[1024,4,128]{0,2,1:T(8,128)(2,1)S(1)} fusion(f32[1024,4,128]{0,2,1:T(8,128)S(1)} %fusion.76, f32[4,1024,1024]{1,2,0:T(8,128)} %get-tuple-element.433, f32[4,1024]{1,0:T(4,128)S(1)} %get-tuple-element.434, f32[1024,4]{0,1:T(4,128)S(1)} %bitcast_maximum_fusion.2, bf16[1024,512]{0,1:T(8,128)(2,1)} %get-tuple-element.491, s32[]{:T(128)S(6)} %select_n.299), kind=kOutput, calls=%fused_computation.18.clone.1 | convolution fusion | flops 1084227584 | bytes 20217860 | tf_op jit(solution)/shard_map/while/body/eval_jaxpr/jtu,ud->tjd/dot_general | solution.py:118
  166.8 1.7 constant_dynamic-slice_fusion.10
  169.4 9.7 %fusion.77 = (f32[4,1024]{1,0:T(4,128)S(1)}, f32[4,1024,1024]{1,2,0:T(8,128)}) fusion(pred[1024,1024]{0,1:T(8,128)(4,1)S(1)} %iota_compare_fusion.2, bf16[1024,4,128]{0,2,1:T(8,128)(2,1)S(1)} %bitcast.97, bf16[1024,512]{0,1:T(8,128)(2,1)S(1)} %get-tuple-element.492, s32[]{:T(128)S(6)} %select_n.299), kind=kOutput, calls=%fused_computation.73.clone.1 | convolution fusion | flops 1090520064 | bytes 19152900 | tf_op jit(solution)/shard_map/while/body/eval_jaxpr/sub | solution.py:115
  181.9 1.3 fusion.76
  183.2 7.4 %fusion.79 = bf16[1024,4,128]{0,2,1:T(8,128)(2,1)S(1)} fusion(f32[1024,4,128]{0,2,1:T(8,128)S(1)} %fusion.76, f32[4,1024,1024]{1,2,0:T(8,128)} %get-tuple-element.433, f32[4,1024]{1,0:T(4,128)S(1)} %get-tuple-element.434, f32[1024,4]{0,1:T(4,128)S(1)} %bitcast_maximum_fusion.2, bf16[1024,512]{0,1:T(8,128)(2,1)} %get-tuple-element.491, s32[]{:T(128)S(6)} %select_n.299), kind=kOutput, calls=%fused_computation.18.clone.1 | convolution fusion | flops 1084227584 | bytes 20217860 | tf_op jit(solution)/shard_map/while/body/eval_jaxpr/jtu,ud->tjd/dot_general | solution.py:118
  192.1 2.6 %broadcast_select_fusion.3 = bf16[512,2048]{1,0:T(8,128)(2,1)S(1)} fusion(pred[]{:T(512)S(6)} %eq.5, bf16[1024,2048]{1,0:T(8,128)(2,1)} %get-tuple-element.256), kind=kLoop, calls=%fused_computation.55 | loop fusion | flops 1048576 | bytes 6291457 | tf_op jit(solution)/shard_map/jit(_where)/select_n | solution.py:138
  195.1 3.9 %collective-permute-done.3 = bf16[512,2048]{1,0:T(8,128)(2,1)S(1)} collective-permute-done((bf16[512,2048]{1,0:T(8,128)(2,1)S(1)}, bf16[512,2048]{1,0:T(8,128)(2,1)S(1)}, u32[]{:S(2)}, u32[]{:S(2)}) %collective-permute-start.3) | collective-permute-done | bytes 2097184 | tf_op jit(solution)/shard_map/ppermute | solution.py:14
  199.4 2.5 %pad_maximum_fusion.1 = bf16[512,4096]{1,0:T(8,128)(2,1)} fusion(bf16[512,2048]{1,0:T(8,128)(2,1)S(1)} %get-tuple-element.344, bf16[512,2048]{1,0:T(8,128)(2,1)S(1)} %get-tuple-element.343), kind=kLoop, calls=%fused_computation.47 | loop fusion | flops 8388608 | bytes 8388608 | tf_op jit(solution)/shard_map/concatenate | solution.py:142
  (109 shorter events, 44.3 us)
Async XLA Ops:
  6.5 61.3 %all-gather.4.cloned.1.call-start = ((), (), s32[]{:S(2)}) async-start(), calls=%async_computation | async-start | bytes 4456448 | tf_op jit(solution)/shard_map/all_gather | solution.py:20
  9.2 2.2 %collective-permute-start = (bf16[512,512]{0,1:T(8,128)(2,1)}, bf16[512,512]{0,1:T(8,128)(2,1)S(1)}, u32[]{:S(2)}, u32[]{:S(2)}) collective-permute-start(bf16[512,512]{0,1:T(8,128)(2,1)} %copy.48), channel_id=1, source_target_pairs={{0,1},{1,0},{2,3},{3,2},{4,5},{5,4},{6,7},{7,6},{8,9},{9,8},{10,11... | collective-permute-start | bytes 1572872 | tf_op jit(solution)/shard_map/ppermute | solution.py:14
  9.9 2.1 collective-permute-start.1
  11.6 1.0 copy-start.1
  13.7 0.7 copy-start.4
  17.6 24.7 %collective-permute-start.2 = (bf16[512,2048]{1,0:T(8,128)(2,1)}, bf16[512,2048]{1,0:T(8,128)(2,1)}, u32[]{:S(2)}, u32[]{:S(2)}) collective-permute-start(bf16[512,2048]{1,0:T(8,128)(2,1)} %constant_dynamic-slice_fusion.4), channel_id=1, source_target_pairs={{0,1},{1,0},{2,3},{3,2},{4,5},{5,4},{6,7},{7,6},{8,9},{9,8},{10,11... | collective-permute-start | bytes 6291464 | tf_op jit(solution)/shard_map/ppermute | solution.py:14
  90.9 2.5 %copy-start.2 = (bf16[1024,512]{0,1:T(8,128)(2,1)}, bf16[1024,512]{0,1:T(8,128)(2,1)S(1)}, u32[]{:S(2)}) copy-start(bf16[1024,512]{0,1:T(8,128)(2,1)S(1)} %get-tuple-element.492) | copy-start | bytes 3145732 | tf_op jit(solution)/shard_map/while
  114.6 1.6 copy-start.3
  116.2 2.5 %copy-start.2 = (bf16[1024,512]{0,1:T(8,128)(2,1)}, bf16[1024,512]{0,1:T(8,128)(2,1)S(1)}, u32[]{:S(2)}) copy-start(bf16[1024,512]{0,1:T(8,128)(2,1)S(1)} %get-tuple-element.492) | copy-start | bytes 3145732 | tf_op jit(solution)/shard_map/while
  139.9 1.6 copy-start.3
  141.5 2.5 %copy-start.2 = (bf16[1024,512]{0,1:T(8,128)(2,1)}, bf16[1024,512]{0,1:T(8,128)(2,1)S(1)}, u32[]{:S(2)}) copy-start(bf16[1024,512]{0,1:T(8,128)(2,1)S(1)} %get-tuple-element.492) | copy-start | bytes 3145732 | tf_op jit(solution)/shard_map/while
  165.2 1.6 copy-start.3
  166.8 2.5 %copy-start.2 = (bf16[1024,512]{0,1:T(8,128)(2,1)}, bf16[1024,512]{0,1:T(8,128)(2,1)S(1)}, u32[]{:S(2)}) copy-start(bf16[1024,512]{0,1:T(8,128)(2,1)S(1)} %get-tuple-element.492) | copy-start | bytes 3145732 | tf_op jit(solution)/shard_map/while
  190.5 1.6 copy-start.3
  192.1 6.8 %copy-start = (bf16[1024,2048]{1,0:T(8,128)(2,1)S(1)}, bf16[1024,2048]{1,0:T(8,128)(2,1)}, u32[]{:S(2)}) copy-start(bf16[1024,2048]{1,0:T(8,128)(2,1)} %get-tuple-element.256) | copy-start | bytes 12582916
  194.7 4.2 %collective-permute-start.3 = (bf16[512,2048]{1,0:T(8,128)(2,1)S(1)}, bf16[512,2048]{1,0:T(8,128)(2,1)S(1)}, u32[]{:S(2)}, u32[]{:S(2)}) collective-permute-start(bf16[512,2048]{1,0:T(8,128)(2,1)S(1)} %broadcast_select_fusion.3), channel_id=1, source_target_pairs={{0,1},{1,0},{2,3},{3,2},{4,5},{5,4},{6,7},{7,6},{8,9},{9,8},{10,11... | collective-permute-start | bytes 6291464 | tf_op jit(solution)/shard_map/ppermute | solution.py:14
Sparse Core Ops, SparseCore 0:
  14.6 53.2 all-gather.3
where the time goes:
time: 210 us; the launch traced here: 209 us
  matrix products  79.4 us (38%)
  other arithmetic  38.4 us (18%)
  local copies, waits for them, and re-layouts  28 us (13%)
  waiting for transfers between devices  24.1 us (11%)
  blocking collectives  23.1 us (11%)
  between operations  13.5 us (6%)
    sub x4, matrix products, head_group(): weights_raw = jnp.exp(scores - row_max)  38.8 us
    dot_general x4, matrix products, head_group(): jnp.einsum('jtu,ud->tjd', weights, value_block, preferred_element_type=jn...  29.5 us
    all_gather x1, blocking collectives, entering(): lax.all_gather(part.astype(kind), axis)  23.1 us
    select_n x32, other arithmetic, step(): return jax.tree.map(lambda a, b: jnp.where(reached, a, b), new, before)  20 us
    all_gather x1, waiting for transfers between devices, entering(): lax.all_gather(part.astype(kind), axis)  18.9 us
    dynamic_slice x8, local copies, waits for them, and re-layouts, head_group(): lax.dynamic_slice_in_dim(query_full, head_index * col_width, col_width, 1)  8.82 us
    dynamic_update_slice x8, local copies, waits for them, and re-layouts, head_group(): lax.dynamic_update_slice_in_dim(output, out_block, head_index * col_width...  6.35 us
    ppermute x4, waiting for transfers between devices, partner(): lax.ppermute(array, axis, [(i, i ^ 1 << distance) for i in range(lax.axis...  5.18 us
  transfers between devices with their start and end apart: 5, of which 4 were waited for; matrix products, arithmetic and copies ran while one was open for 6% of the time, Pallas kernels for 0%

commit v1 on v0

v1 whole, which is shorter than its diff:
```python
import functools
import math

import jax
import jax.numpy as jnp
from jax import lax
from jax.experimental import pallas as pl
from jax.experimental.pallas import tpu as pltpu
from jax.sharding import PartitionSpec as P

QH = 32
KVH = 8
DH = 128
GROUP = QH // KVH
HALF = KVH // 2
WIDTH = GROUP * DH
NORM_ROWS = 16
BLOCK = 256
MESH = pl.DeviceIdType.MESH
LAST = (((1,), (1,)), ((), ()))
FIRST = (((0,), (0,)), ((), ()))


def features(x):
    x = x.astype(jnp.float32)
    return jnp.where(x > 0, x + 1.0, jnp.exp(x)).astype(jnp.bfloat16)


def kernel(
    steps, rows,
    q_ref, k_ref, v_ref, out_ref,
    q_s, k_s, v_s, loc_s, o_s, total, before, snd, rcv, memaug,
    own_sem, q_send, q_recv, kv_send, kv_recv, m_send, m_recv, o_own, o_send, o_recv,
):
    me = lax.axis_index("seg")
    side = me % 2
    seg = me // 2
    other = 1 - side
    mate = me + 1 - 2 * side
    peers, bits = [], []
    for t in range(steps):
        bit = (seg // 2**t) % 2
        bits.append(bit)
        peers.append((seg + (1 - 2 * bit) * 2**t) * 2 + side)

    barrier = pltpu.get_barrier_semaphore()
    for d in [mate] + peers:
        pl.semaphore_signal(barrier, inc=1, device_id={"seg": d}, device_id_type=MESH)

    my_rows = pl.ds(pl.multiple_of(side * rows, rows), rows)
    mate_rows = pl.ds(pl.multiple_of(other * rows, rows), rows)

    def cols(which, width, g=0, size=None):
        start = which * (HALF * width) + g * width
        return pl.ds(pl.multiple_of(start, 128), size or width)

    own = []
    for n, (src, dst) in enumerate(((k_ref, k_s), (v_ref, v_s))):
        own.append(pltpu.make_async_copy(
            src.at[:, cols(side, DH, 0, HALF * DH)], dst.at[my_rows, :], own_sem.at[n]))
    for g in range(HALF):
        own.append(pltpu.make_async_copy(
            q_ref.at[:, cols(side, WIDTH, g)], q_s.at[g, my_rows, :], own_sem.at[2 + g]))
    for c in own:
        c.start()
    pl.semaphore_wait(barrier, 1 + steps)

    def remote(src, dst, s, r, dev):
        return pltpu.make_async_remote_copy(
            src_ref=src, dst_ref=dst, send_sem=s, recv_sem=r,
            device_id={"seg": dev}, device_id_type=MESH)

    kv = []
    for n, (src, dst) in enumerate(((k_ref, k_s), (v_ref, v_s))):
        kv.append(remote(src.at[:, cols(other, DH, 0, HALF * DH)], dst.at[my_rows, :],
                         kv_send.at[n], kv_recv.at[n], mate))
    qs = []
    for g in range(HALF):
        qs.append(remote(q_ref.at[:, cols(other, WIDTH, g)], q_s.at[g, my_rows, :],
                         q_send.at[g], q_recv.at[g], mate))
    for c in kv + qs:
        c.start()

    own[0].wait()
    own[1].wait()
    kv[0].wait_recv()
    kv[1].wait_recv()

    seg_rows = 2 * rows
    ones_rows = jnp.ones((NORM_ROWS, seg_rows), jnp.bfloat16)
    for g in range(HALF):
        kf = features(k_s[:, g * DH:(g + 1) * DH])
        total[g, 0:DH, :] = lax.dot_general(
            kf, v_s[:, g * DH:(g + 1) * DH], FIRST, preferred_element_type=jnp.float32)
        total[g, DH:, :] = jnp.dot(ones_rows, kf, preferred_element_type=jnp.float32)
    before[...] = jnp.zeros_like(before)

    def send_total(t):
        snd[t] = total[...].astype(jnp.bfloat16)
        copy = remote(snd.at[t], rcv.at[t], m_send.at[t], m_recv.at[t], peers[t])
        copy.start()
        return copy

    sums = []
    if steps:
        sums.append(send_total(0))

    def take_total(t):
        sums[t].wait_recv()
        got = rcv[t].astype(jnp.float32)
        before[...] += got * bits[t].astype(jnp.float32)
        if t + 1 < steps:
            total[...] += got
            sums.append(send_total(t + 1))

    scale = math.log2(math.e) / math.sqrt(DH)
    lower = (lax.broadcasted_iota(jnp.int32, (BLOCK, BLOCK), 1)
             <= lax.broadcasted_iota(jnp.int32, (BLOCK, BLOCK), 0))

    def local(g):
        def head(j, _):
            at = pl.ds(pl.multiple_of(j * DH, DH), DH)
            for i in range(seg_rows // BLOCK):
                lo = i * BLOCK
                here = slice(lo, lo + BLOCK)
                q = q_s[g, here, at]
                gc = slice(g * DH, (g + 1) * DH)
                ones = jnp.ones((BLOCK, DH), jnp.bfloat16)
                sd = lax.dot_general(q, k_s[here, gc], LAST, preferred_element_type=jnp.float32)
                sd = jnp.where(lower, sd, -1e30)
                top = jnp.max(sd, axis=-1, keepdims=True)
                if i:
                    so = lax.dot_general(
                        q, k_s[0:lo, gc], LAST, preferred_element_type=jnp.float32)
                    top = jnp.maximum(top, jnp.max(so, axis=-1, keepdims=True))
                pd = jnp.exp2((sd - top) * scale).astype(jnp.bfloat16)
                acc = jnp.dot(pd, jnp.concatenate([v_s[here, gc], ones], 1),
                              preferred_element_type=jnp.float32)
                if i:
                    po = jnp.exp2((so - top) * scale).astype(jnp.bfloat16)
                    ones = jnp.ones((lo, DH), jnp.bfloat16)
                    acc += jnp.dot(po, jnp.concatenate([v_s[0:lo, gc], ones], 1),
                                   preferred_element_type=jnp.float32)
                loc_s[g, here, at] = acc[:, :DH] / acc[:, DH:]
            return 0
        lax.fori_loop(0, GROUP, head, 0)

    def prepare():
        for g in range(HALF):
            full = before[g]
            norm = jnp.broadcast_to(full[DH:DH + 1, :], (DH, DH)).T
            both = jnp.concatenate([full[:DH, :], norm], 1)
            high = both.astype(jnp.bfloat16)
            memaug[g, 0:DH, :] = high
            memaug[g, DH:, :] = (both - high.astype(jnp.float32)).astype(jnp.bfloat16)

    outs = []

    def finish(g):
        def head(j, _):
            at = pl.ds(pl.multiple_of(j * DH, DH), DH)
            for i in range(seg_rows // BLOCK):
                here = slice(i * BLOCK, (i + 1) * BLOCK)
                qf = features(q_s[g, here, at])
                r = jnp.dot(jnp.concatenate([qf, qf], 1), memaug[g],
                            preferred_element_type=jnp.float32)
                read = r[:, :DH] / jnp.maximum(r[:, DH:], 1.0)
                o_s[g, here, at] = (0.5 * (loc_s[g, here, at] + read)).astype(jnp.bfloat16)
            return 0
        lax.fori_loop(0, GROUP, head, 0)
        there = out_ref.at[:, cols(side, WIDTH, g)]
        far = remote(o_s.at[g, mate_rows, :], there, o_send.at[g], o_recv.at[g], mate)
        far.start()
        near = pltpu.make_async_copy(o_s.at[g, my_rows, :], there, o_own.at[g])
        near.start()
        outs.append((far, near))

    ready = HALF - 1
    each = -(-steps // ready)
    taken = 0
    for g in range(HALF):
        own[2 + g].wait()
        qs[g].wait_recv()
        local(g)
        while taken < min(steps, (g + 1) * each):
            take_total(taken)
            taken += 1
        if g == ready - 1:
            prepare()
            for h in range(ready):
                finish(h)
        if g >= ready:
            finish(g)

    for c in kv + qs + sums:
        c.wait_send()
    for far, near in outs:
        near.wait()
        far.wait()


def solution(mesh):
    count = mesh.shape["seg"] // 2
    steps = count.bit_length() - 1
    assert count == 2**steps

    def on_device(queries, keys, values):
        rows = queries.shape[0]
        seg_rows = 2 * rows
        bf16, f32 = jnp.bfloat16, jnp.float32
        dma = pltpu.SemaphoreType.DMA
        slots = max(steps, 1)
        sums = (HALF, DH + NORM_ROWS, DH)
        return pl.pallas_call(
            functools.partial(kernel, steps, rows),
            out_shape=jax.ShapeDtypeStruct(queries.shape, bf16),
            in_specs=[pl.BlockSpec(memory_space=pl.ANY)] * 3,
            out_specs=pl.BlockSpec(memory_space=pl.ANY),
            scratch_shapes=[
                pltpu.VMEM((HALF, seg_rows, WIDTH), bf16),
                pltpu.VMEM((seg_rows, HALF * DH), bf16),
                pltpu.VMEM((seg_rows, HALF * DH), bf16),
                pltpu.VMEM((HALF, seg_rows, WIDTH), f32),
                pltpu.VMEM((HALF, seg_rows, WIDTH), bf16),
                pltpu.VMEM(sums, f32),
                pltpu.VMEM(sums, f32),
                pltpu.VMEM((slots,) + sums, bf16),
                pltpu.VMEM((slots,) + sums, bf16),
                pltpu.VMEM((HALF, 2 * DH, 2 * DH), bf16),
                dma((2 + HALF,)),
                dma((HALF,)), dma((HALF,)),
                dma((2,)), dma((2,)),
                dma((slots,)), dma((slots,)),
                dma((HALF,)), dma((HALF,)), dma((HALF,)),
            ],
            compiler_params=pltpu.CompilerParams(
                collective_id=0, has_side_effects=True, vmem_limit_bytes=52 * 2**20),
            cost_estimate=pl.CostEstimate(
                flops=4 * seg_rows * seg_rows * QH // 2 * DH,
                bytes_accessed=20 * rows * QH * DH // 2,
                transcendentals=seg_rows * seg_rows * QH // 4),
        )(queries, keys, values)

    return jax.shard_map(
        on_device,
        mesh=mesh,
        in_specs=(P(("groups", "seg"), None),) * 3,
        out_specs=P(("groups", "seg"), None),
        check_vma=False,
    )
```

time: 210 us -> 51.1 us (0.24)
  matrix products: 79.4 us -> 0 us
  Pallas kernels: 0 us -> 45 us
  other arithmetic: 38.4 us -> 0 us
  waiting for transfers between devices: 24.1 us -> 0 us
  blocking collectives: 23.1 us -> 0 us
  local copies, waits for them, and re-layouts: 28 us -> 5.92 us
  between operations: 13.5 us -> 0.01 us
    pallas_call x0 -> x1, Pallas kernels: none -> 45 us  [on_device(): pl.pallas_call(functools.partial(kernel, steps, rows), out_shape=jax.Shap...]
    dot_general x13 -> x0, matrix products: 40.6 us -> none  [the longest x4 29.5 us: head_group(): jnp.einsum('jtu,ud->tjd', weights, value_block, preferred_element_type=jn...]
    sub x4 -> x0, matrix products: 38.8 us -> none  [head_group(): weights_raw = jnp.exp(scores - row_max)]
    select_n x37 -> x0, other arithmetic: 27.1 us -> none  [the longest x32 20 us: step(): return jax.tree.map(lambda a, b: jnp.where(reached, a, b), new, before)]
    all_gather x1 -> x0, blocking collectives: 23.1 us -> none  [entering(): lax.all_gather(part.astype(kind), axis)]
    all_gather x1 -> x0, waiting for transfers between devices: 18.9 us -> none  [entering(): lax.all_gather(part.astype(kind), axis)]
    dynamic_slice x12 -> x0, local copies, waits for them, and re-layouts: 13.7 us -> none  [the longest x8 8.82 us: head_group(): lax.dynamic_slice_in_dim(query_full, head_index * col_width, col_width, 1)]
    dynamic_update_slice x9 -> x0, local copies, waits for them, and re-layouts: 6.37 us -> none  [the longest x8 6.35 us: head_group(): lax.dynamic_update_slice_in_dim(output, out_block, head_index * col_width...]
  transfers between devices with their start and end apart: 5 -> 0, of which waited for: 4 -> 0; matrix products, arithmetic and copies ran while one was open for 6% -> 0% of each run, Pallas kernels for 0% -> 0%
where the time goes in v1:
time: 51.1 us; the launch traced here: 50.9 us
  Pallas kernels  45 us (88%)
  local copies, waits for them, and re-layouts  5.92 us (12%)
    pallas_call x1, Pallas kernels, on_device(): pl.pallas_call(functools.partial(kernel, steps, rows), out_shape=jax.Shap...  45 us
    unnamed x3, local copies, waits for them, and re-layouts  5.92 us

profile of v1, /device:TPU:0, one launch (start us, length us, event | category | flops | bytes accessed | tf_op | source)
XLA Modules:
  0.0 50.9 jit_solution(7825133523243012934)
XLA Ops:
  0.0 0.0 copy-start
  0.0 1.2 %copy-done = bf16[512,1024]{1,0:T(8,128)(2,1)S(1)} copy-done((bf16[512,1024]{1,0:T(8,128)(2,1)S(1)}, bf16[512,1024]{1,0:T(8,128)(2,1)}, u32[]{:S(2)}) %copy-start) | copy-done | bytes 1048600
  1.2 45.0 %shard_map.37 = bf16[512,4096]{1,0:T(8,128)(2,1)} custom-call(bf16[512,4096]{1,0:T(8,128)(2,1)} %q_ref.1, bf16[512,1024]{1,0:T(8,128)(2,1)S(1)} %copy-done, bf16[512,1024]{1,0:T(8,128)(2,1)} %v_ref.1), custom_call_target="tpu_custom_call" | custom-call | flops 8589934592 | bytes 20971520 | tf_op jit(solution)/shard_map/pallas_call | solution.py:214
  46.2 4.7 %copy.5 = bf16[512,4096]{1,0:T(8,128)(2,1)} copy(bf16[512,4096]{1,0:T(8,128)(2,1)} %shard_map.37) | data formatting | bytes 8388608
Async XLA Ops:
  0.0 1.2 %copy-start = (bf16[512,1024]{1,0:T(8,128)(2,1)S(1)}, bf16[512,1024]{1,0:T(8,128)(2,1)}, u32[]{:S(2)}) copy-start(bf16[512,1024]{1,0:T(8,128)(2,1)} %k_ref.1) | copy-start | bytes 3145732

commit v2 on v1

--- a/solution.py
+++ b/solution.py
@@ -16,6 +16,7 @@
 WIDTH = GROUP * DH
 NORM_ROWS = 16
 BLOCK = 256
+PAIR = 2
 MESH = pl.DeviceIdType.MESH
 LAST = (((1,), (1,)), ((), ()))
 FIRST = (((0,), (0,)), ((), ()))
@@ -81,19 +82,24 @@
     for c in kv + qs:
         c.start()
 
+    seg_rows = 2 * rows
+    ones_rows = jnp.ones((NORM_ROWS, rows), jnp.bfloat16)
+
+    def add_terms(part):
+        for g in range(HALF):
+            kf = features(k_s[part, g * DH:(g + 1) * DH])
+            total[g, 0:DH, :] += lax.dot_general(
+                kf, v_s[part, g * DH:(g + 1) * DH], FIRST, preferred_element_type=jnp.float32)
+            total[g, DH:, :] += jnp.dot(ones_rows, kf, preferred_element_type=jnp.float32)
+
+    before[...] = jnp.zeros_like(before)
+    total[...] = jnp.zeros_like(total)
     own[0].wait()
     own[1].wait()
+    add_terms(my_rows)
     kv[0].wait_recv()
     kv[1].wait_recv()
-
-    seg_rows = 2 * rows
-    ones_rows = jnp.ones((NORM_ROWS, seg_rows), jnp.bfloat16)
-    for g in range(HALF):
-        kf = features(k_s[:, g * DH:(g + 1) * DH])
-        total[g, 0:DH, :] = lax.dot_general(
-            kf, v_s[:, g * DH:(g + 1) * DH], FIRST, preferred_element_type=jnp.float32)
-        total[g, DH:, :] = jnp.dot(ones_rows, kf, preferred_element_type=jnp.float32)
-    before[...] = jnp.zeros_like(before)
+    add_terms(mate_rows)
 
     def send_total(t):
         snd[t] = total[...].astype(jnp.bfloat16)
@@ -114,16 +120,17 @@
             sums.append(send_total(t + 1))
 
     scale = math.log2(math.e) / math.sqrt(DH)
-    lower = (lax.broadcasted_iota(jnp.int32, (BLOCK, BLOCK), 1)
-             <= lax.broadcasted_iota(jnp.int32, (BLOCK, BLOCK), 0))
+    shape = (PAIR * BLOCK, BLOCK)
+    lower = (lax.broadcasted_iota(jnp.int32, shape, 1)
+             <= lax.broadcasted_iota(jnp.int32, shape, 0) % BLOCK)
 
     def local(g):
-        def head(j, _):
-            at = pl.ds(pl.multiple_of(j * DH, DH), DH)
+        def heads(j, _):
+            ats = [pl.ds(pl.multiple_of((j * PAIR + a) * DH, DH), DH) for a in range(PAIR)]
             for i in range(seg_rows // BLOCK):
                 lo = i * BLOCK
                 here = slice(lo, lo + BLOCK)
-                q = q_s[g, here, at]
+                q = jnp.concatenate([q_s[g, here, at] for at in ats], 0)
                 gc = slice(g * DH, (g + 1) * DH)
                 ones = jnp.ones((BLOCK, DH), jnp.bfloat16)
                 sd = lax.dot_general(q, k_s[here, gc], LAST, preferred_element_type=jnp.float32)
@@ -141,9 +148,11 @@
                     ones = jnp.ones((lo, DH), jnp.bfloat16)
                     acc += jnp.dot(po, jnp.concatenate([v_s[0:lo, gc], ones], 1),
                                    preferred_element_type=jnp.float32)
-                loc_s[g, here, at] = acc[:, :DH] / acc[:, DH:]
+                for a in range(PAIR):
+                    to = pl.ds(pl.multiple_of((j * PAIR + a) * 2 * DH, 2 * DH), 2 * DH)
+                    loc_s[g, here, to] = acc[a * BLOCK:(a + 1) * BLOCK]
             return 0
-        lax.fori_loop(0, GROUP, head, 0)
+        lax.fori_loop(0, GROUP // PAIR, heads, 0)
 
     def prepare():
         for g in range(HALF):
@@ -156,21 +165,27 @@
 
     outs = []
 
-    def finish(g):
+    def finish_rows(g, start):
         def head(j, _):
             at = pl.ds(pl.multiple_of(j * DH, DH), DH)
-            for i in range(seg_rows // BLOCK):
-                here = slice(i * BLOCK, (i + 1) * BLOCK)
+            for i in range(rows // BLOCK):
+                here = pl.ds(pl.multiple_of(start + i * BLOCK, BLOCK), BLOCK)
                 qf = features(q_s[g, here, at])
                 r = jnp.dot(jnp.concatenate([qf, qf], 1), memaug[g],
                             preferred_element_type=jnp.float32)
-                read = r[:, :DH] / jnp.maximum(r[:, DH:], 1.0)
-                o_s[g, here, at] = (0.5 * (loc_s[g, here, at] + read)).astype(jnp.bfloat16)
+                near = loc_s[g, here, pl.ds(pl.multiple_of(j * 2 * DH, 2 * DH), 2 * DH)]
+                row, den = near[:, DH:], jnp.maximum(r[:, DH:], 1.0)
+                both = (near[:, :DH] * den + r[:, :DH] * row) / (row * den)
+                o_s[g, here, at] = (0.5 * both).astype(jnp.bfloat16)
             return 0
         lax.fori_loop(0, GROUP, head, 0)
+
+    def finish(g):
         there = out_ref.at[:, cols(side, WIDTH, g)]
+        finish_rows(g, other * rows)
         far = remote(o_s.at[g, mate_rows, :], there, o_send.at[g], o_recv.at[g], mate)
         far.start()
+        finish_rows(g, side * rows)
         near = pltpu.make_async_copy(o_s.at[g, my_rows, :], there, o_own.at[g])
         near.start()
         outs.append((far, near))
@@ -199,6 +214,21 @@
         far.wait()
 
 
+def pass_on(parts, src_ref, dst_ref, held, in_sem, out_sem):
+    size = held.shape[0] // parts
+    loads, stores = [], []
+    for n in range(parts):
+        part = slice(n * size, (n + 1) * size)
+        loads.append(pltpu.make_async_copy(src_ref.at[part, :], held.at[part, :], in_sem.at[n]))
+        stores.append(pltpu.make_async_copy(held.at[part, :], dst_ref.at[part, :], out_sem.at[n]))
+        loads[n].start()
+    for n in range(parts):
+        loads[n].wait()
+        stores[n].start()
+    for n in range(parts):
+        stores[n].wait()
+
+
 def solution(mesh):
     count = mesh.shape["seg"] // 2
     steps = count.bit_length() - 1
@@ -211,7 +241,7 @@
         dma = pltpu.SemaphoreType.DMA
         slots = max(steps, 1)
         sums = (HALF, DH + NORM_ROWS, DH)
-        return pl.pallas_call(
+        joined = pl.pallas_call(
             functools.partial(kernel, steps, rows),
             out_shape=jax.ShapeDtypeStruct(queries.shape, bf16),
             in_specs=[pl.BlockSpec(memory_space=pl.ANY)] * 3,
@@ -220,7 +250,7 @@
                 pltpu.VMEM((HALF, seg_rows, WIDTH), bf16),
                 pltpu.VMEM((seg_rows, HALF * DH), bf16),
                 pltpu.VMEM((seg_rows, HALF * DH), bf16),
-                pltpu.VMEM((HALF, seg_rows, WIDTH), f32),
+                pltpu.VMEM((HALF, seg_rows, 2 * WIDTH), f32),
                 pltpu.VMEM((HALF, seg_rows, WIDTH), bf16),
                 pltpu.VMEM(sums, f32),
                 pltpu.VMEM(sums, f32),
@@ -234,12 +264,23 @@
                 dma((HALF,)), dma((HALF,)), dma((HALF,)),
             ],
             compiler_params=pltpu.CompilerParams(
-                collective_id=0, has_side_effects=True, vmem_limit_bytes=52 * 2**20),
+                collective_id=0, has_side_effects=True, vmem_limit_bytes=60 * 2**20),
             cost_estimate=pl.CostEstimate(
                 flops=4 * seg_rows * seg_rows * QH // 2 * DH,
                 bytes_accessed=20 * rows * QH * DH // 2,
                 transcendentals=seg_rows * seg_rows * QH // 4),
         )(queries, keys, values)
+        parts = math.gcd(rows // 16, 16)
+        return pl.pallas_call(
+            functools.partial(pass_on, parts),
+            out_shape=jax.ShapeDtypeStruct(joined.shape, bf16),
+            in_specs=[pl.BlockSpec(memory_space=pl.ANY)],
+            out_specs=pl.BlockSpec(memory_space=pl.ANY),
+            scratch_shapes=[pltpu.VMEM(joined.shape, bf16), dma((parts,)), dma((parts,))],
+            compiler_params=pltpu.CompilerParams(vmem_limit_bytes=60 * 2**20),
+            cost_estimate=pl.CostEstimate(
+                flops=0, bytes_accessed=4 * joined.size, transcendentals=0),
+        )(joined)
 
     return jax.shard_map(
         on_device,

time: 51.1 us -> 45.9 us (0.90)
  local copies, waits for them, and re-layouts: 5.92 us -> 0 us
  Pallas kernels: 45 us -> 45.7 us
    unnamed x3 -> x0, local copies, waits for them, and re-layouts: 5.92 us -> none
    pallas_call x0 -> x1, Pallas kernels: none -> 3.85 us  [on_device(): pl.pallas_call(functools.partial(pass_on, parts), out_shape=jax.ShapeDtyp...]
    pallas_call x1, Pallas kernels: 45 us -> 41.8 us  [on_device(): pl.pallas_call(functools.partial(kernel, steps, rows), out_shape=jax.Shap...]
where the time goes in v2:
time: 45.9 us; the launch traced here: 45.7 us
  Pallas kernels  45.7 us (100%)
    pallas_call x1, Pallas kernels, on_device(): pl.pallas_call(functools.partial(kernel, steps, rows), out_shape=jax.Shap...  41.8 us
    pallas_call x1, Pallas kernels, on_device(): pl.pallas_call(functools.partial(pass_on, parts), out_shape=jax.ShapeDtyp...  3.85 us

profile of v2, /device:TPU:0, one launch (start us, length us, event | category | flops | bytes accessed | tf_op | source)
XLA Modules:
  0.0 45.7 jit_solution(5494308515065296261)
XLA Ops:
  0.0 41.8 %shard_map.37.src_ref = bf16[512,4096]{1,0:T(8,128)(2,1)} custom-call(bf16[512,4096]{1,0:T(8,128)(2,1)} %q_ref.1, bf16[512,1024]{1,0:T(8,128)(2,1)} %k_ref.1, bf16[512,1024]{1,0:T(8,128)(2,1)} %v_ref.1), custom_call_target="tpu_custom_call" | custom-call | flops 8589934592 | bytes 20971520 | tf_op jit(solution)/shard_map/pallas_call | solution.py:244
  41.9 3.9 %shard_map.38 = bf16[512,4096]{1,0:T(8,128)(2,1)} custom-call(bf16[512,4096]{1,0:T(8,128)(2,1)} %shard_map.37.src_ref), custom_call_target="tpu_custom_call" | custom-call | bytes 8388608 | tf_op jit(solution)/shard_map/pallas_call | solution.py:274
